TPU v7x, 1024 devices: a whole 4x4x32 slice. The times are simulated.
1024 devices in a mesh: fsdp: 256 (over z, y, core), tp: 4 (over x).
Axes of the slice: x: 4, y: 4, z: 32, core: 2. Of those that a mesh axis runs over, the one named last changes fastest.
Arguments:
- momentum: float32 [28672, 8192], P('fsdp', 'tp'), may hold values from -200 to 200
- gradient: bfloat16 [28672, 8192], P('fsdp', 'tp'), may hold values from -24 to 24
- basis: float32 [8192, 256], P('tp'), may hold values from -0.0625 to 0.0625
Outputs:
- new_momentum: float32 [28672, 8192], P('fsdp', 'tp')
- q_next: float32 [8192, 256], P(('tp', 'fsdp'))
- direction: float32 [28672, 8192], P('fsdp', 'tp')
All inputs are finite; a program needn't handle non-finite values.
Results may differ from a plain program's by a relative error of at most 0.0003.
Values sent between devices are 32-bit elements; how exact they have to be, the bound alone decides.
No kernel may reach another device: no remote copies, remote signals or barrier semaphores. Data moves between devices by JAX's collectives and lax.ppermute only.
A program may use at most 32 MiB of HBM per device.

v0:
```python
import math

import jax
import jax.numpy as jnp
from jax import lax
from jax.sharding import PartitionSpec as P

D = 8192
FF = 28672
RANK = 256


def shards(momentum, gradient, basis):
    highest = lax.Precision.HIGHEST
    buffer = momentum + gradient.astype(jnp.float32)
    partial_left = jnp.dot(buffer, basis, precision=highest, preferred_element_type=jnp.float32)
    left_factor = lax.psum(partial_left, "tp")
    local_gram = lax.dot_general(
        left_factor,
        left_factor,
        (((0,), (0,)), ((), ())),
        precision=highest,
        preferred_element_type=jnp.float32,
    )
    gram = lax.psum(local_gram, "fsdp")
    gram = gram + 1.0 * FF * jnp.eye(RANK, dtype=jnp.float32)
    factor = jnp.linalg.cholesky(gram)
    orthonormal = lax.linalg.triangular_solve(
        factor, left_factor, left_side=False, lower=True, transpose_a=True
    )
    partial_right = lax.dot_general(
        buffer,
        orthonormal,
        (((0,), (0,)), ((), ())),
        precision=highest,
        preferred_element_type=jnp.float32,
    )
    right_rows = lax.psum_scatter(partial_right, "fsdp", scatter_dimension=0, tiled=True)
    dir_scale = math.sqrt(FF * D / RANK)
    squares = lax.psum(jnp.sum(right_rows * right_rows, axis=0), ("fsdp", "tp"))
    col_norms = jnp.sqrt(squares + 1e-06)
    q_rows = right_rows / col_norms[None, :]
    stacked_left = jnp.stack([dir_scale * orthonormal, 0.05 * orthonormal * col_norms[None, :]])
    q_whole = lax.all_gather(q_rows, "fsdp", axis=0, tiled=True)
    products = jnp.einsum(
        "smr,cr->smc", stacked_left, q_whole, precision=highest, preferred_element_type=jnp.float32
    )
    new_momentum = buffer - products[1]
    direction = products[0]
    return (new_momentum, q_rows, direction)


def solution(mesh):
    return jax.shard_map(
        shards,
        mesh=mesh,
        in_specs=(P("fsdp", "tp"), P("fsdp", "tp"), P("tp", None)),
        out_specs=(P("fsdp", "tp"), P(("tp", "fsdp"), None), P("fsdp", "tp")),
        check_vma=False,
    )
```

profile of v0, /device:TPU:1, one launch (start us, length us, event | category | flops | bytes accessed | tf_op | source)
XLA Modules:
  0.0 1704.3 jit_solution(10951803458203687893)
XLA Ops:
  7.2 0.0 copy-start
  7.2 0.0 all-reduce.4.cloned.1.call-start
  7.2 1.5 copy-done
  8.8 3.1 fusion.4
  11.8 0.0 all-reduce.4.cloned.1.call-update
  11.9 0.0 all-reduce.6.cloned.1.call-start
  11.9 83.1 %all-reduce.4.cloned.1.call-done = f32[112,256]{1,0:T(8,128)} async-done(((f32[112,256]{1,0:T(8,128)}), f32[112,256]{1,0:T(8,128)}) %all-reduce.4.cloned.1.call-update) | async-done | bytes 114704 | tf_op jit(solution)/shard_map/psum | solution.py:17
  95.0 2.1 fusion.24
  97.1 0.0 all-reduce.6.cloned.1.call-update
  97.1 0.0 reduce-scatter.2.cloned.1.call-start
  97.2 628.2 %all-reduce.6.cloned.1.call-done = f32[256,256]{0,1:T(8,128)} async-done(((f32[256,256]{0,1:T(8,128)}), f32[256,256]{0,1:T(8,128)}) %all-reduce.6.cloned.1.call-update) | async-done | bytes 262160 | tf_op jit(solution)/shard_map/psum | solution.py:25
  725.3 1.0 select_add_fusion
  726.3 0.1 copy.7
  726.5 1.0 fusion.5
  727.5 11.7 cholesky.49
  739.2 0.1 copy.8
  739.3 0.0 copy-start.3
  739.3 9.8 custom-call.14
  749.1 0.2 fusion.17
  749.3 0.9 convolution_subtract_fusion
  750.2 0.0 copy-start.1
  750.3 0.1 copy.9
  750.3 12.6 cholesky.103
  763.0 0.1 copy.10
  763.1 0.7 compare_reduce_fusion
  765.3 0.1 triangular_solve.67
  765.3 5.7 while.1
  765.5 0.6 fusion.33
  766.1 1.4 dynamic-slice.7
  767.5 0.1 copy.15
  767.6 0.6 bitcast_dynamic-update-slice_fusion.2
  768.3 0.6 fusion.33
  768.9 1.4 dynamic-slice.7
  770.3 0.1 copy.15
  770.4 0.6 bitcast_dynamic-update-slice_fusion.2
  771.0 21.1 %custom-call.15 = f32[2,128,128]{1,2,0:T(8,128)} custom-call(f32[2,128,128]{2,1,0:T(8,128)} %get-tuple-element.10), custom_call_target="InvertDiagBlocksLowerTriangular" | custom-call | tf_op jit(solution)/shard_map/triangular_solve | solution.py:28
  792.1 0.0 copy-done.3
  792.1 1.0 fusion.16
  793.2 0.2 convolution_subtract_fusion.1
  793.4 1.0 fusion.14
  794.4 0.0 copy-done.1
  794.4 4.2 fusion.3
  798.7 0.0 reduce-scatter.2.cloned.1.call-update
  798.7 0.0 all-gather.2.cloned.1.call-start
  798.7 466.3 %reduce-scatter.2.cloned.1.call-done = f32[8,256]{1,0:T(8,128)} async-done(((f32[2048,256]{1,0:T(8,128)}), f32[8,256]{1,0:T(8,128)}) %reduce-scatter.2.cloned.1.call-update) | async-done | bytes 8208 | tf_op jit(solution)/shard_map/reduce_scatter | solution.py:38
  1265.0 0.7 multiply_reduce_fusion
  1265.7 177.0 %psum.23 = f32[256]{0:T(256)S(1)} all-reduce(f32[256]{0:T(256)S(1)} %multiply_reduce_fusion), channel_id=1, replica_groups=mesh['fsdp'=256,'tp'=4] {'fsdp','tp'}, use_global_device_ids=true, to_apply=%region_8.9 | all-reduce | flops 256 | bytes 2048 | tf_op jit(solution)/shard_map/psum | solution.py:40
  1442.7 1.3 broadcast_divide_fusion
  1444.1 0.0 all-gather.2.cloned.1.call-update
  1444.1 247.8 %all-gather.2.cloned.1.call-done = f32[2048,256]{1,0:T(8,128)} async-done(((f32[8,256]{1,0:T(8,128)}), f32[2048,256]{1,0:T(8,128)}) %all-gather.2.cloned.1.call-update) | async-done | bytes 2097168 | tf_op jit(solution)/shard_map/all_gather | solution.py:44
  1691.9 0.0 copy-start.2
  1691.9 3.8 fusion
  1695.7 1.0 slice_bitcast_fusion
  1696.7 0.0 copy-done.2
  1696.7 1.1 fusion.2
  (13 shorter events, 0.2 us)
Async XLA Ops:
  7.2 1.6 copy-start
  7.2 87.8 %all-reduce.4.cloned.1.call-start = ((), (), s32[]{:S(2)}) async-start(), calls=%async_computation.1 | async-start | bytes 229376 | tf_op jit(solution)/shard_map/psum | solution.py:17
  11.9 713.5 %all-reduce.6.cloned.1.call-start = ((), (), s32[]{:S(2)}) async-start(), calls=%async_computation.2 | async-start | bytes 524288 | tf_op jit(solution)/shard_map/psum | solution.py:25
  97.1 1167.9 %reduce-scatter.2.cloned.1.call-start = ((), (), s32[]{:S(2)}) async-start(), calls=%async_computation.3 | async-start | bytes 2105344 | tf_op jit(solution)/shard_map/reduce_scatter | solution.py:38
  739.3 52.9 %copy-start.3 = (f32[112,256]{1,0:T(8,128)S(1)}, f32[112,256]{1,0:T(8,128)}, u32[]{:S(2)}) copy-start(f32[112,256]{1,0:T(8,128)} %all-reduce.4.cloned.1.call-done) | copy-start | bytes 344068
  750.2 44.2 %copy-start.1 = (f32[112,2048]{1,0:T(8,128)S(1)}, f32[112,2048]{1,0:T(8,128)}, u32[]{:S(2)}) copy-start(f32[112,2048]{1,0:T(8,128)} %param.3) | copy-start | bytes 2752516
  798.7 893.2 %all-gather.2.cloned.1.call-start = ((), (), s32[]{:S(2)}) async-start(), calls=%async_computation.4 | async-start | bytes 2105344 | tf_op jit(solution)/shard_map/all_gather | solution.py:44
  1691.9 4.8 copy-start.2
Sparse Core Ops, SparseCore 0:
  12.0 82.9 all-reduce.3
  99.4 625.8 all-reduce.5
  798.8 466.1 reduce-scatter.1
  1444.2 247.6 all-gather.1
where the time goes:
time: 1710 us; the launch traced here: 1700 us
  waiting for transfers between devices  1430 us (84%)
  blocking collectives  177 us (10%)
  other arithmetic  61.2 us (4%)
    psum x1, waiting for transfers between devices, shards(): gram = lax.psum(local_gram, 'fsdp')  628 us
    reduce_scatter x1, waiting for transfers between devices, shards(): lax.psum_scatter(partial_right, 'fsdp', scatter_dimension=0, tiled=True)  466 us
    all_gather x1, waiting for transfers between devices, shards(): q_whole = lax.all_gather(q_rows, 'fsdp', axis=0, tiled=True)  248 us
    psum x1, blocking collectives, shards(): squares = lax.psum(jnp.sum(right_rows * right_rows, axis=0), ('fsdp', 'tp'))  177 us
    psum x1, waiting for transfers between devices, shards(): left_factor = lax.psum(partial_left, 'tp')  83.1 us
    another operation x6, other arithmetic, shards(): factor = jnp.linalg.cholesky(gram)  34.9 us
  transfers between devices with their start and end apart: 4, of which 4 were waited for; matrix products, arithmetic and copies ran while one was open for 0% of the time, Pallas kernels for 0%

commit v1 on v0

v1 whole, which is shorter than its diff:
```python
import math

import jax
import jax.numpy as jnp
from jax import lax
from jax.experimental import pallas as pl
from jax.experimental.pallas import tpu as pltpu
from jax.sharding import Mesh, PartitionSpec as P

D = 8192
FF = 28672
RANK = 256
SIZES = {"zh": 4, "zl": 8, "y": 4, "c": 2, "tp": 4}
ROWS = ("zh", "zl", "y", "c")
HIGHEST = lax.Precision.HIGHEST
F32 = jnp.float32
FIRST = (((0,), (0,)), ((), ()))
LAST = (((1,), (1,)), ((), ()))
STEPS = 2
SIDE = 64
GROUP = 8
PARAMS = pltpu.CompilerParams(vmem_limit_bytes=12 * 2**20)


def dot(a, b, dims):
    return lax.dot_general(a, b, dims, precision=HIGHEST, preferred_element_type=F32)


def exchange(blocks, axis):
    return lax.all_to_all(blocks, axis, 0, 0, tiled=True)


def left_products(momentum_hbm, gradient_hbm, basis_hbm, out_ref, buffer_ref, gradient_ref, basis_ref, sems):
    part = buffer_ref.shape[1] // STEPS
    copies = []
    for i in range(STEPS):
        cols = pl.ds(i * part, part)
        pairs = (
            (basis_hbm.at[cols, :], basis_ref.at[cols, :]),
            (momentum_hbm.at[:, cols], buffer_ref.at[:, cols]),
            (gradient_hbm.at[:, cols], gradient_ref.at[:, cols]),
        )
        copies.append([pltpu.make_async_copy(src, dst, sems.at[i, k]) for k, (src, dst) in enumerate(pairs)])
        for copy in copies[i]:
            copy.start()
    total = None
    for i in range(STEPS):
        for copy in copies[i]:
            copy.wait()
        cols = slice(i * part, (i + 1) * part)
        buffer = buffer_ref[:, cols] + gradient_ref[:, cols].astype(F32)
        buffer_ref[:, cols] = buffer
        product = dot(buffer, basis_ref[cols, :], (((1,), (0,)), ((), ())))
        total = product if total is None else total + product
    for i in range(out_ref.shape[0]):
        out_ref[i] = total


def local_products(core_ref, parts_ref, buffer_ref, left_ref, keep_ref, send_ref):
    first = core_ref[0] == 0
    left = (parts_ref[0] + parts_ref[1]) + (parts_ref[2] + parts_ref[3])
    left_ref[...] = left

    def put(y, zl, tile, blocks):
        keep_ref[y, zl, tile * 8 : tile * 8 + 8, :] = jnp.where(first, blocks[0], blocks[1])
        send_ref[y, zl, tile * 8 : tile * 8 + 8, :] = jnp.where(first, blocks[1], blocks[0])

    gram = dot(left, left, FIRST)
    for y in range(4):
        for zl in range(8):
            at = (y * 8 + zl) // 2 * 8
            lanes = slice(zl % 2 * 128, zl % 2 * 128 + 128)
            blocks = [gram[c * 128 + at : c * 128 + at + 8, lanes] for c in range(2)]
            put(y, zl, 8, blocks)
    for zh in range(4):
        cols = slice(zh * 512, (zh + 1) * 512)
        rows = dot(buffer_ref[:, cols], left, FIRST).reshape(8, 4, 2, 8, RANK)
        for y in range(4):
            for zl in range(8):
                for half in range(2):
                    lanes = slice(half * 128, half * 128 + 128)
                    put(y, zl, zh * 2 + half, [rows[zl, y, 0][:, lanes], rows[zl, y, 1][:, lanes]])


def add(a_ref, b_ref, out_ref):
    out_ref[...] = a_ref[...] + b_ref[...]


def sum_first(parts_ref, out_ref):
    total = parts_ref[0]
    for i in range(1, parts_ref.shape[0]):
        total += parts_ref[i]
    out_ref[...] = total


def sum_and_copy(parts_ref, out_ref):
    total = parts_ref[0]
    for i in range(1, parts_ref.shape[0]):
        total += parts_ref[i]
    for i in range(out_ref.shape[0]):
        out_ref[i] = total


def copies(block_ref, out_ref):
    block = block_ref[...]
    for i in range(out_ref.shape[0]):
        out_ref[i] = block


def inverse_of_block(block, eye):
    tile = jnp.concatenate([block, eye], axis=1)
    full = tile.shape
    row_id = lax.broadcasted_iota(jnp.int32, full, 0)

    def wide(v):
        return jnp.broadcast_to(v, full)

    def flat(v):
        return jnp.broadcast_to(v, (1, full[1]))

    for j in range(0, SIDE, GROUP):
        rows = [tile[j + a : j + a + 1, :] for a in range(GROUP)]
        cols = [wide(tile[:, j + a : j + a + 1]) for a in range(GROUP)]
        p = {(a, b): flat(rows[a][:, j + b : j + b + 1]) for a in range(GROUP) for b in range(a, GROUP)}
        for a in range(GROUP):
            inv = 1.0 / p[a, a]
            for b in range(a + 1, GROUP):
                ratio = p[a, b] * inv
                for d in range(b, GROUP):
                    p[b, d] = p[b, d] - ratio * p[a, d]
                rows[b] = rows[b] - ratio * rows[a]
                cols[b] = cols[b] - cols[a] * wide(ratio)
            tile = tile - jnp.where(row_id > j + a, cols[a], 0.0) * wide(rows[a] * inv)
    pivots = jnp.sum(jnp.where(eye > 0.0, tile[:, :SIDE], 0.0), axis=1, keepdims=True)
    return tile[:, SIDE:] * lax.rsqrt(pivots)


def solve(core_ref, mine_ref, other_ref, left_ref, ortho_ref, right_ref, squares_ref, work):
    halves_of = ((core_ref[0], mine_ref), (1 - core_ref[0], other_ref))
    for c, ref in halves_of:
        for y in range(4):
            for zl in range(8):
                at = pl.ds(pl.multiple_of(c * 128 + (y * 8 + zl) // 2 * 8, 8), 8)
                work[at, zl % 2 * 128 : zl % 2 * 128 + 128] = ref[y, zl, 64:72, :]
    r = lax.broadcasted_iota(jnp.int32, (RANK, RANK), 0)
    c = lax.broadcasted_iota(jnp.int32, (RANK, RANK), 1)
    work[...] += jnp.where(r == c, 1.0 * FF, 0.0)
    r = lax.broadcasted_iota(jnp.int32, (SIDE, SIDE), 0)
    c = lax.broadcasted_iota(jnp.int32, (SIDE, SIDE), 1)
    eye = jnp.where(r == c, 1.0, 0.0)
    lane = lax.broadcasted_iota(jnp.int32, (1, RANK), 1)
    for lo in range(0, RANK, SIDE):
        hi = lo + SIDE
        rows = work[lo:hi, :]
        inverse = inverse_of_block(rows[:, lo:hi], eye)
        inside = (lane >= lo) & (lane < hi)
        pieces = [jnp.zeros((SIDE, lo), F32)] * (lo > 0) + [eye] + [jnp.zeros((SIDE, RANK - hi), F32)] * (hi < RANK)
        rows = jnp.where(inside, jnp.concatenate(pieces, axis=1), rows)
        rows = dot(inverse, rows, (((1,), (0,)), ((), ())))
        work[lo:hi, :] = jnp.where(lane < hi, rows, 0.0)
        if hi < RANK:
            work[hi:, :] = jnp.where(inside, 0.0, work[hi:, :]) - dot(rows[:, hi:], rows, FIRST)
    inverse = work[...]
    ortho_ref[...] = dot(left_ref[...], inverse, LAST)
    squares = jnp.zeros((1, RANK), F32)
    for c, ref in halves_of:
        for y in range(4):
            raw = ref[y, :, 0:64, :].reshape(8, 4, 2, 8, 128)
            raw = jnp.concatenate([raw[:, :, 0], raw[:, :, 1]], axis=-1).reshape(8 * 32, RANK)
            right = dot(raw, inverse, LAST)
            squares += jnp.sum(right * right, axis=0, keepdims=True)
            right = right.reshape(8, 4, 8, RANK)
            for zl in range(8):
                for zh in range(4):
                    at = pl.multiple_of(zh * 512 + (zl * 4 + y) * 16 + c * 8, 8)
                    right_ref[pl.ds(at, 8), :] = right[zl, zh]
    squares_ref[...] = jnp.broadcast_to(squares, squares_ref.shape)


def halves(value):
    high = value.astype(jnp.bfloat16)
    return high, (value - high.astype(F32)).astype(jnp.bfloat16)


def outer(a_high, a_low, b):
    b_high, b_low = b

    def product(x, y):
        return lax.dot_general(x, y, LAST, preferred_element_type=F32)

    return product(a_high, b_high) + (product(a_high, b_low) + product(a_low, b_high))


def finish(place_ref, squares_ref, buffer_ref, ortho_ref, right_ref, momentum_ref, direction_ref, q_ref):
    squares = (squares_ref[0] + squares_ref[1]) + (squares_ref[2] + squares_ref[3])
    norms = jnp.sqrt(squares + 1e-06)
    own = pl.ds(pl.multiple_of(place_ref[0] * 8, 8), 8)
    q_ref[...] = right_ref[own, :] / norms
    ortho = ortho_ref[...]
    high, low = halves(ortho)
    scaled_high, scaled_low = halves(math.sqrt(FF * D / RANK) * ortho / norms[0:1, :])
    for i in range(8):
        cols = slice(i * 256, (i + 1) * 256)
        right = halves(right_ref[cols, :])
        momentum_ref[:, cols] = buffer_ref[:, cols] - 0.05 * outer(high, low, right)
        direction_ref[:, cols] = outer(scaled_high, scaled_low, right)


def shape(*dims):
    return jax.ShapeDtypeStruct(dims, F32)


def call(kernel, out_shape, *args, scalars=0, **options):
    specs = [pl.BlockSpec(memory_space=pltpu.SMEM)] * scalars
    specs += [pl.BlockSpec(memory_space=pltpu.VMEM)] * (len(args) - scalars)
    return pl.pallas_call(
        kernel, out_shape=out_shape, in_specs=specs, compiler_params=PARAMS, name=kernel.__name__, **options
    )(*args)


def shards(momentum, gradient, basis):
    height, width = momentum.shape
    core = lax.axis_index("c").astype(jnp.int32).reshape(1)
    place = lax.axis_index(ROWS).astype(jnp.int32).reshape(1)
    partial_left, buffer = pl.pallas_call(
        left_products,
        in_specs=[pl.BlockSpec(memory_space=pltpu.HBM)] * 3,
        out_specs=[pl.BlockSpec(memory_space=pltpu.VMEM)] * 2,
        out_shape=[shape(4, height, RANK), shape(height, width)],
        scratch_shapes=[
            pltpu.VMEM(gradient.shape, gradient.dtype),
            pltpu.VMEM(basis.shape, F32),
            pltpu.SemaphoreType.DMA((STEPS, 3)),
        ],
        compiler_params=pltpu.CompilerParams(vmem_limit_bytes=58 * 2**20),
        name="left_products",
    )(momentum, gradient, basis)
    parts = exchange(partial_left, "tp")
    block = shape(4, 8, 72, 128)
    left, keep, send = call(
        local_products, [shape(height, RANK), block, block], core, parts, buffer, scalars=1
    )

    swap = ((0, 1), (1, 0))
    sums = call(add, block, keep, lax.ppermute(send, "c", swap))
    sums = call(sum_first, shape(8, 72, 128), exchange(sums, "y"))
    sums = call(sum_and_copy, shape(4, 72, 128), exchange(sums, "zl"))
    sums = call(sum_and_copy, shape(8, 72, 128), exchange(sums, "zh"))
    sums = call(copies, block, exchange(sums, "zl"))
    mine = exchange(sums, "y")
    other = lax.ppermute(mine, "c", swap)

    ortho, right, squares = call(
        solve,
        [shape(height, RANK), shape(width, RANK), shape(4, 8, RANK)],
        core, mine, other, left,
        scalars=1,
        scratch_shapes=[pltpu.VMEM((RANK, RANK), F32)],
    )
    squares = exchange(squares, "tp")
    new_momentum, direction, q_rows = call(
        finish,
        [shape(height, width), shape(height, width), shape(8, RANK)],
        place, squares, buffer, ortho, right,
        scalars=1,
    )
    return (new_momentum, q_rows, direction)


def solution(mesh):
    fine = Mesh(mesh.devices.reshape([SIZES[a] for a in ROWS] + [SIZES["tp"]]), ROWS + ("tp",))
    return jax.shard_map(
        shards,
        mesh=fine,
        in_specs=(P(ROWS, "tp"), P(ROWS, "tp"), P("tp", None)),
        out_specs=(P(ROWS, "tp"), P(("tp",) + ROWS, None), P(ROWS, "tp")),
        check_vma=False,
    )
```

time: 1710 us -> 191 us (0.11)
  waiting for transfers between devices: 1430 us -> 15.6 us
  other arithmetic: 61.2 us -> 0 us
  blocking collectives: 177 us -> 119 us
  starting transfers between devices: 0.16 us -> 34 us
  Pallas kernels: 0 us -> 21.2 us
    psum x2 -> x0, waiting for transfers between devices: 711 us -> none  [the longest x1 628 us: shards(): gram = lax.psum(local_gram, 'fsdp')]
    reduce_scatter x1 -> x0, waiting for transfers between devices: 466 us -> none  [shards(): lax.psum_scatter(partial_right, 'fsdp', scatter_dimension=0, tiled=True)]
    all_gather x1 -> x0, waiting for transfers between devices: 248 us -> none  [shards(): q_whole = lax.all_gather(q_rows, 'fsdp', axis=0, tiled=True)]
    psum x1 -> x0, blocking collectives: 177 us -> none  [shards(): squares = lax.psum(jnp.sum(right_rows * right_rows, axis=0), ('fsdp', 'tp'))]
    all_to_all x0 -> x5, blocking collectives: none -> 119 us  [exchange(): return lax.all_to_all(blocks, axis, 0, 0, tiled=True)]
    another operation x9 -> x0, other arithmetic: 56.1 us -> none  [the longest x6 34.9 us: shards(): factor = jnp.linalg.cholesky(gram)]
    ppermute x0 -> x2, starting transfers between devices: none -> 25.7 us  [the longest x1 15.8 us: shards(): sums = call(add, block, keep, lax.ppermute(send, 'c', swap))]
    pallas_call x0 -> x9, Pallas kernels: none -> 21.2 us  [the longest x8 17.2 us: call(): pl.pallas_call(kernel, out_shape=out_shape, in_specs=specs, compiler_para...]
where the time goes in v1:
time: 191 us; the launch traced here: 190 us
  blocking collectives  119 us (62%)
  starting transfers between devices  34 us (18%)
  Pallas kernels  21.2 us (11%)
  waiting for transfers between devices  15.6 us (8%)
    all_to_all x5, blocking collectives, exchange(): return lax.all_to_all(blocks, axis, 0, 0, tiled=True)  119 us
    pallas_call x8, Pallas kernels, call(): pl.pallas_call(kernel, out_shape=out_shape, in_specs=specs, compiler_para...  17.2 us
    ppermute x1, starting transfers between devices, shards(): sums = call(add, block, keep, lax.ppermute(send, 'c', swap))  15.8 us
    all_to_all x2, waiting for transfers between devices, exchange(): return lax.all_to_all(blocks, axis, 0, 0, tiled=True)  10.8 us
    ppermute x1, starting transfers between devices, shards(): other = lax.ppermute(mine, 'c', swap)  9.92 us
    all_to_all x2, starting transfers between devices, exchange(): return lax.all_to_all(blocks, axis, 0, 0, tiled=True)  8.25 us
    pallas_call x1, Pallas kernels, shards(): pl.pallas_call(left_products, in_specs=[pl.BlockSpec(memory_space=pltpu.H...  3.98 us
  transfers between devices with their start and end apart: 4, of which 4 were waited for; matrix products, arithmetic and copies ran while one was open for 0% of the time, Pallas kernels for 0%

profile of v1, /device:TPU:1, one launch (start us, length us, event | category | flops | bytes accessed | tf_op | source)
XLA Modules:
  0.0 190.1 jit_solution(7317332976568244573)
XLA Ops:
  0.6 4.0 %left_products.1 = (f32[4,112,256]{2,1,0:T(8,128)}, f32[112,2048]{1,0:T(8,128)}) custom-call(f32[112,2048]{1,0:T(8,128)} %momentum_hbm.1, bf16[112,2048]{1,0:T(8,128)(2,1)} %gradient_hbm.1, f32[2048,256]{1,0:T(8,128)} %basis_hbm.1), custom_call_target="tpu_custom_call" | custom-call | tf_op jit(solution)/shard_map/left_products/pallas_call | solution.py:225
  4.6 0.0 copy-start
  4.6 5.0 %all-to-all-start = ((f32[4,112,256]{2,1,0:T(8,128)}), f32[4,112,256]{2,1,0:T(8,128)S(1)}, u32[]{:S(2)}, u32[]{:S(2)}) async-start(f32[4,112,256]{2,1,0:T(8,128)} %get-tuple-element.14), calls=%async_computation | async-start | bytes 917504 | tf_op jit(solution)/shard_map/all_to_all | solution.py:30
  9.6 6.6 %all-to-all-done.parts_ref = f32[4,112,256]{2,1,0:T(8,128)S(1)} async-done(((f32[4,112,256]{2,1,0:T(8,128)}), f32[4,112,256]{2,1,0:T(8,128)S(1)}, u32[]{:S(2)}, u32[]{:S(2)}) %all-to-all-start) | async-done | bytes 458784 | tf_op jit(solution)/shard_map/all_to_all | solution.py:30
  16.2 0.0 copy-done
  16.2 2.1 %local_products.1 = (f32[112,256]{1,0:T(8,128)S(1)}, f32[4,8,72,128]{3,2,1,0:T(8,128)S(1)}, f32[4,8,72,128]{3,2,1,0:T(8,128)S(1)}) custom-call(s32[1]{0:T(128)} %bitcast.1.core_ref, f32[4,112,256]{2,1,0:T(8,128)S(1)} %all-to-all-done.parts_ref, f32[112,2048]{1,0:T(8,128)S(1)} %copy-done), custom_call_target="tpu_custom_call" | custom-call | tf_op jit(solution)/shard_map/local_products/pallas_call | solution.py:216
  18.3 15.8 %collective-permute-start = (f32[4,8,72,128]{3,2,1,0:T(8,128)S(1)}, f32[4,8,72,128]{3,2,1,0:T(8,128)S(1)}, u32[]{:S(2)}, u32[]{:S(2)}) collective-permute-start(f32[4,8,72,128]{3,2,1,0:T(8,128)S(1)} %get-tuple-element.17), channel_id=1, source_target_pairs={{0,4},{4,0},{1,5},{5,1},{2,6},{6,2},{3,7},{7,3},{8,12},{12,8},{9,1... | collective-permute-start | bytes 3538952 | tf_op jit(solution)/shard_map/ppermute | solution.py:245
  34.1 2.5 %collective-permute-done.b_ref = f32[4,8,72,128]{3,2,1,0:T(8,128)S(1)} collective-permute-done((f32[4,8,72,128]{3,2,1,0:T(8,128)S(1)}, f32[4,8,72,128]{3,2,1,0:T(8,128)S(1)}, u32[]{:S(2)}, u32[]{:S(2)}) %collective-permute-start) | collective-permute-done | bytes 1179680 | tf_op jit(solution)/shard_map/ppermute | solution.py:245
  36.5 0.1 add.13
  36.7 18.7 %all_to_all.35.parts_ref = f32[4,8,72,128]{3,2,1,0:T(8,128)S(1)} all-to-all(f32[4,8,72,128]{3,2,1,0:T(8,128)S(1)} %add.13), channel_id=1, replica_groups=mesh['zh'=4,'zl'=8,'y'=4,'c'=2,'tp'=4] {'y'}, dimensions={0} | all-to-all | bytes 2359296 | tf_op jit(solution)/shard_map/all_to_all | solution.py:30
  55.3 0.1 sum_first.1
  55.4 18.7 %all_to_all.36.parts_ref = f32[8,72,128]{2,1,0:T(8,128)S(1)} all-to-all(f32[8,72,128]{2,1,0:T(8,128)S(1)} %sum_first.1), channel_id=1, replica_groups=mesh['zh'=4,'zl'=8,'y'=4,'c'=2,'tp'=4] {'zl'}, dimensions={0} | all-to-all | bytes 589824 | tf_op jit(solution)/shard_map/all_to_all | solution.py:30
  74.1 42.2 %all_to_all.37.parts_ref = f32[4,72,128]{2,1,0:T(8,128)S(1)} all-to-all(f32[4,72,128]{2,1,0:T(8,128)S(1)} %sum_and_copy.2), channel_id=1, replica_groups=mesh['zh'=4,'zl'=8,'y'=4,'c'=2,'tp'=4] {'zh'}, dimensions={0} | all-to-all | bytes 294912 | tf_op jit(solution)/shard_map/all_to_all | solution.py:30
  116.3 26.2 %all_to_all.38.block_ref = f32[8,72,128]{2,1,0:T(8,128)S(1)} all-to-all(f32[8,72,128]{2,1,0:T(8,128)S(1)} %sum_and_copy.3), channel_id=1, replica_groups=mesh['zh'=4,'zl'=8,'y'=4,'c'=2,'tp'=4] {'zl'}, dimensions={0} | all-to-all | bytes 589824 | tf_op jit(solution)/shard_map/all_to_all | solution.py:30
  142.6 0.1 copies.1
  142.6 12.9 %all_to_all.39.mine_ref = f32[4,8,72,128]{3,2,1,0:T(8,128)S(1)} all-to-all(f32[4,8,72,128]{3,2,1,0:T(8,128)S(1)} %copies.1), channel_id=1, replica_groups=mesh['zh'=4,'zl'=8,'y'=4,'c'=2,'tp'=4] {'y'}, dimensions={0} | all-to-all | bytes 2359296 | tf_op jit(solution)/shard_map/all_to_all | solution.py:30
  155.5 9.9 %collective-permute-start.1 = (f32[4,8,72,128]{3,2,1,0:T(8,128)S(1)}, f32[4,8,72,128]{3,2,1,0:T(8,128)S(1)}, u32[]{:S(2)}, u32[]{:S(2)}) collective-permute-start(f32[4,8,72,128]{3,2,1,0:T(8,128)S(1)} %all_to_all.39.mine_ref), channel_id=1, source_target_pairs={{0,4},{4,0},{1,5},{5,1},{2,6},{6,2},{3,7},{7,3},{8,12},{12,8},{9,1... | collective-permute-start | bytes 3538952 | tf_op jit(solution)/shard_map/ppermute | solution.py:251
  165.4 2.3 %collective-permute-done.1.other_ref = f32[4,8,72,128]{3,2,1,0:T(8,128)S(1)} collective-permute-done((f32[4,8,72,128]{3,2,1,0:T(8,128)S(1)}, f32[4,8,72,128]{3,2,1,0:T(8,128)S(1)}, u32[]{:S(2)}, u32[]{:S(2)}) %collective-permute-start.1) | collective-permute-done | bytes 1179680 | tf_op jit(solution)/shard_map/ppermute | solution.py:251
  167.7 11.5 %solve.1 = (f32[112,256]{1,0:T(8,128)S(1)}, f32[2048,256]{1,0:T(8,128)S(1)}, f32[4,8,256]{2,1,0:T(8,128)}) custom-call(s32[1]{0:T(128)} %bitcast.1.core_ref, f32[4,8,72,128]{3,2,1,0:T(8,128)S(1)} %all_to_all.39.mine_ref, f32[4,8,72,128]{3,2,1,0:T(8,128)S(1)} %collective-permute-done.1.other_ref, f32[112,256]{1,0:T(8,128)S(1)} %get-tuple-element.18.left_ref), custom_call_target="tpu_custom_call" | custom-call | tf_op jit(solution)/shard_map/solve/pallas_call | solution.py:216
  179.2 3.3 %all-to-all-start.6 = ((f32[4,8,256]{2,1,0:T(8,128)}), f32[4,8,256]{2,1,0:T(8,128)S(1)}, u32[]{:S(2)}, u32[]{:S(2)}) async-start(f32[4,8,256]{2,1,0:T(8,128)} %get-tuple-element.19), calls=%async_computation.6 | async-start | bytes 65536 | tf_op jit(solution)/shard_map/all_to_all | solution.py:30
  182.5 4.3 %all-to-all-done.6.squares_ref = f32[4,8,256]{2,1,0:T(8,128)S(1)} async-done(((f32[4,8,256]{2,1,0:T(8,128)}), f32[4,8,256]{2,1,0:T(8,128)S(1)}, u32[]{:S(2)}, u32[]{:S(2)}) %all-to-all-start.6) | async-done | bytes 32800 | tf_op jit(solution)/shard_map/all_to_all | solution.py:30
  186.8 3.3 %finish.1 = (f32[112,2048]{1,0:T(8,128)}, f32[112,2048]{1,0:T(8,128)}, f32[8,256]{1,0:T(8,128)}) custom-call(s32[1]{0:T(128)} %bitcast.place_ref, f32[4,8,256]{2,1,0:T(8,128)S(1)} %all-to-all-done.6.squares_ref, f32[112,2048]{1,0:T(8,128)S(1)} %copy-done, f32[112,256]{1,0:T(8,128)S(1)} %get-tuple-element.20.ortho_ref, ...), custom_call_target="tpu_custom_call" | custom-call | tf_op jit(solution)/shard_map/finish/pallas_call | solution.py:216
  (2 shorter events, 0.0 us)
Async XLA Ops:
  4.6 11.6 %copy-start = (f32[112,2048]{1,0:T(8,128)S(1)}, f32[112,2048]{1,0:T(8,128)}, u32[]{:S(2)}) copy-start(f32[112,2048]{1,0:T(8,128)} %get-tuple-element.15.buffer_ref) | copy-start | bytes 2752516
  4.6 11.6 %all-to-all-start = ((f32[4,112,256]{2,1,0:T(8,128)}), f32[4,112,256]{2,1,0:T(8,128)S(1)}, u32[]{:S(2)}, u32[]{:S(2)}) async-start(f32[4,112,256]{2,1,0:T(8,128)} %get-tuple-element.14), calls=%async_computation | async-start | bytes 917504 | tf_op jit(solution)/shard_map/all_to_all | solution.py:30
  18.3 18.3 %collective-permute-start = (f32[4,8,72,128]{3,2,1,0:T(8,128)S(1)}, f32[4,8,72,128]{3,2,1,0:T(8,128)S(1)}, u32[]{:S(2)}, u32[]{:S(2)}) collective-permute-start(f32[4,8,72,128]{3,2,1,0:T(8,128)S(1)} %get-tuple-element.17), channel_id=1, source_target_pairs={{0,4},{4,0},{1,5},{5,1},{2,6},{6,2},{3,7},{7,3},{8,12},{12,8},{9,1... | collective-permute-start | bytes 3538952 | tf_op jit(solution)/shard_map/ppermute | solution.py:245
  155.5 12.2 %collective-permute-start.1 = (f32[4,8,72,128]{3,2,1,0:T(8,128)S(1)}, f32[4,8,72,128]{3,2,1,0:T(8,128)S(1)}, u32[]{:S(2)}, u32[]{:S(2)}) collective-permute-start(f32[4,8,72,128]{3,2,1,0:T(8,128)S(1)} %all_to_all.39.mine_ref), channel_id=1, source_target_pairs={{0,4},{4,0},{1,5},{5,1},{2,6},{6,2},{3,7},{7,3},{8,12},{12,8},{9,1... | collective-permute-start | bytes 3538952 | tf_op jit(solution)/shard_map/ppermute | solution.py:251
  179.2 7.5 %all-to-all-start.6 = ((f32[4,8,256]{2,1,0:T(8,128)}), f32[4,8,256]{2,1,0:T(8,128)S(1)}, u32[]{:S(2)}, u32[]{:S(2)}) async-start(f32[4,8,256]{2,1,0:T(8,128)} %get-tuple-element.19), calls=%async_computation.6 | async-start | bytes 65536 | tf_op jit(solution)/shard_map/all_to_all | solution.py:30
